TPU v7x, 32 devices: a whole 2x2x4 slice. The times are simulated.
32 devices in a mesh: grp: 2 (over x), chan: 16 (over z, y, core).
Axes of the slice: x: 2, y: 2, z: 4, core: 2. Of those that a mesh axis runs over, the one named last changes fastest.
Arguments:
- voltages: int32 [512, 2, 2, 32, 1024], P(('grp', 'chan')), parts along dimension 0, may hold values from -127 to 127
- scales: int32 [512, 1024], P(('grp', 'chan')), parts along dimension 0, may hold values from 1 to 8
- feed_positions: float32 [3, 1024], replicated, may hold values from -8 to 8
- beam_directions: float32 [3, 128], replicated, may hold values from -1 to 1
- dm_trials: int32 [256], replicated, may hold values from 0 to 255, each once
Outputs:
- dedispersed: float32 [256, 32, 256], P(None, ('grp', 'chan')), parts along dimension 1
There are 2 independent parts, one for each index of `grp`. A program takes and returns all parts, laid end to end along the dimension named above; an argument that names none is the same for every part. Nothing has to cross between parts.
Inputs may be any that keep to these rules, and one draw needn't show every extreme that they name: dm_trials holds each number of 0 to 255 once.
All inputs are finite; a program needn't handle non-finite values.
Results may differ from a plain program's by a relative error of at most 0.0046.
Values may be sent and summed in bfloat16 or wider, within the bound.
No kernel may reach another device: no remote copies, remote signals or barrier semaphores. Data moves between devices by JAX's collectives and lax.ppermute only.
A program may use at most 320 MiB of HBM per device.

v0:
```python
import math
import jax
import jax.numpy as jnp
from jax import lax
from jax.sharding import PartitionSpec as P

MAXD = 15
TWO_PI = 6.283185307179586
POWER_SCALE = 1.0 / 67108864.0


def passed_along(value, axis, steps):
    count = lax.axis_size(axis)
    leading, last = (max(0, -steps), min(count, count - steps))
    return lax.ppermute(value, axis, [(source, source + steps) for source in range(leading, last)])


def geometry_delay(feed_positions, beam_directions):
    total = feed_positions[0][:, None] * beam_directions[0][None, :]
    total = total + feed_positions[1][:, None] * beam_directions[1][None, :]
    return total + feed_positions[2][:, None] * beam_directions[2][None, :]


def channel_flat(volt_chan, scale_chan, cosine, sine):
    scale_col = scale_chan.astype(jnp.float32)[:, None]
    weight_pair = jnp.concatenate([scale_col * cosine, scale_col * sine], axis=1).astype(
        jnp.bfloat16
    )
    row_block = volt_chan.astype(jnp.bfloat16).reshape(-1, volt_chan.shape[-1])
    product = jnp.dot(row_block, weight_pair, preferred_element_type=jnp.float32)
    beam_count = cosine.shape[1]
    product = product.reshape(2, 2, volt_chan.shape[2], 2, beam_count)
    real_part = product[0, :, :, 0] - product[1, :, :, 1]
    imag_part = product[0, :, :, 1] + product[1, :, :, 0]
    detected = (
        real_part[0] * real_part[0]
        + imag_part[0] * imag_part[0]
        + (real_part[1] * real_part[1] + imag_part[1] * imag_part[1])
    )
    detected = detected * POWER_SCALE
    return (detected - jnp.mean(detected, axis=0, keepdims=True)).astype(jnp.bfloat16)


def delay_table(dm_trials, chan_total, trial_count):
    chan_ids = jnp.arange(chan_total, dtype=jnp.int32)
    upper = jnp.int32(chan_total) + chan_ids
    sweeps = jnp.int32(256 * chan_total * chan_total) // (upper * upper) - jnp.int32(64)
    return (
        dm_trials[:, None] * sweeps[None, :] * jnp.int32(MAXD + 1) // jnp.int32(trial_count * 192)
    )


def dedisperse(extended, onehots, time_steps, scaling):
    chan_total = extended.shape[0]
    beam_items = extended.shape[2]
    accumulate = jnp.zeros((onehots[0].shape[0], time_steps * beam_items), jnp.float32)
    for shift_step in range(MAXD + 1):
        segment = extended[:, shift_step : shift_step + time_steps, :].reshape(
            chan_total, time_steps * beam_items
        )
        accumulate = accumulate + jnp.dot(
            onehots[shift_step], segment, preferred_element_type=jnp.float32
        )
    return (accumulate * scaling).reshape(onehots[0].shape[0], time_steps, beam_items)


def local(voltages, scales, feed_positions, beam_directions, dm_trials):
    chan_local = voltages.shape[0]
    window = voltages.shape[3]
    groups = lax.axis_size("chan")
    half_groups = groups // 2
    chan_total = groups * chan_local
    beam_count = beam_directions.shape[1]
    block_beams = beam_count // half_groups
    time_steps = window // 2
    trial_count = dm_trials.shape[0]
    scaling = 1.0 / math.sqrt(chan_total)
    geometry = geometry_delay(feed_positions, beam_directions)
    first_chan = lax.axis_index("chan") * chan_local
    frequency = first_chan.astype(jnp.float32) / chan_total + 1.0
    phase = TWO_PI * frequency * geometry
    cosine = jnp.cos(phase)
    sine = jnp.sin(phase)
    flat = lax.map(lambda items: channel_flat(items[0], items[1], cosine, sine), (voltages, scales))
    delays = delay_table(dm_trials, chan_total, trial_count)
    onehots = [(delays == shift_step).astype(jnp.bfloat16) for shift_step in range(MAXD + 1)]
    outgoing = flat.reshape(chan_local, 2, time_steps, half_groups, block_beams)
    outgoing = outgoing.transpose(1, 3, 0, 2, 4).reshape(
        groups, chan_local, time_steps, block_beams
    )
    arrived = lax.all_to_all(outgoing, "chan", split_axis=0, concat_axis=0, tiled=True)
    arrived_block = arrived.reshape(chan_total, time_steps, arrived.shape[3])
    tail_rows = passed_along(arrived_block[:, :MAXD, :], "chan", -half_groups)
    extended = jnp.concatenate([arrived_block, tail_rows], axis=1)
    result = dedisperse(extended, onehots, time_steps, scaling)
    return result.reshape(trial_count, 1, time_steps * block_beams)


def solution(mesh):
    return jax.shard_map(
        local,
        mesh=mesh,
        in_specs=(
            P(("grp", "chan"), None, None, None, None),
            P(("grp", "chan"), None),
            P(),
            P(),
            P(),
        ),
        out_specs=P(None, ("grp", "chan"), None),
        check_vma=False,
    )
```

profile of v0, /device:TPU:0, one launch (start us, length us, event | category | flops | bytes accessed | tf_op | source)
XLA Modules:
  0.0 111.3 jit_solution(13977786807538412760)
XLA Ops:
  1.7 71.5 %while.12 = (s32[]{:T(128)}, bf16[16,32,128]{2,1,0:T(8,128)(2,1)S(1)}, s32[16,2,2,32,1024]{4,3,2,1,0:T(8,128)}, s32[16,1024]{1,0:T(8,128)}, f32[128]{0:T(128)S(1...) while((s32[]{:T(128)}, ...), condition=%wide.region_2.3_spmd.clone.clone, body=%wide.region_0.2_spmd.clone.clone.sunk | while | flops 69661696 | bytes 3083917 | solution.py:84
  2.4 2.2 %fusion.189 = (bf16[1024,128]{0,1:T(8,128)(2,1)S(1)}, bf16[1024,128]{0,1:T(8,128)(2,1)S(1)}) fusion(f32[128]{0:T(128)S(1)} %get-tuple-element.290, f32[1024]{0:T(1024)S(1)} %get-tuple-element.291, f32[128]{0:T(128)S(1)} %get-tuple-element.288, f32[1024]{0:T(1024)S(1)} %get-tuple-element.289, f32[128]{0:T(128)S(1)} %get-tuple-element.286, ...), kind=kLoop, calls=%fused_computation.6.clone.1 | loop fusion | flops 1310720 | bytes 542212 | tf_op jit(solution)/shard_map/convert
  4.7 1.4 %fusion.190 = f32[2,2,32,2,128]{4,2,3,1,0:T(8,128)S(1)} fusion(bf16[2,128,1024,1,1]{2,1,0,4,3:T(8,128)(2,1)S(1)} %bitcast.78, s32[16,2,2,32,1024]{4,3,2,1,0:T(8,128)} %get-tuple-element.284, s32[]{:T(128)S(6)} %copy.19), kind=kOutput, calls=%fused_computation.10.clone.1 | convolution fusion | flops 67239936 | bytes 1179652 | tf_op jit(solution)/shard_map/while/body/eval_jaxpr/dot_general | solution.py:30
  6.9 2.2 %fusion.189 = (bf16[1024,128]{0,1:T(8,128)(2,1)S(1)}, bf16[1024,128]{0,1:T(8,128)(2,1)S(1)}) fusion(f32[128]{0:T(128)S(1)} %get-tuple-element.290, f32[1024]{0:T(1024)S(1)} %get-tuple-element.291, f32[128]{0:T(128)S(1)} %get-tuple-element.288, f32[1024]{0:T(1024)S(1)} %get-tuple-element.289, f32[128]{0:T(128)S(1)} %get-tuple-element.286, ...), kind=kLoop, calls=%fused_computation.6.clone.1 | loop fusion | flops 1310720 | bytes 542212 | tf_op jit(solution)/shard_map/convert
  11.4 2.2 %fusion.189 = (bf16[1024,128]{0,1:T(8,128)(2,1)S(1)}, bf16[1024,128]{0,1:T(8,128)(2,1)S(1)}) fusion(f32[128]{0:T(128)S(1)} %get-tuple-element.290, f32[1024]{0:T(1024)S(1)} %get-tuple-element.291, f32[128]{0:T(128)S(1)} %get-tuple-element.288, f32[1024]{0:T(1024)S(1)} %get-tuple-element.289, f32[128]{0:T(128)S(1)} %get-tuple-element.286, ...), kind=kLoop, calls=%fused_computation.6.clone.1 | loop fusion | flops 1310720 | bytes 542212 | tf_op jit(solution)/shard_map/convert
  15.9 2.2 %fusion.189 = (bf16[1024,128]{0,1:T(8,128)(2,1)S(1)}, bf16[1024,128]{0,1:T(8,128)(2,1)S(1)}) fusion(f32[128]{0:T(128)S(1)} %get-tuple-element.290, f32[1024]{0:T(1024)S(1)} %get-tuple-element.291, f32[128]{0:T(128)S(1)} %get-tuple-element.288, f32[1024]{0:T(1024)S(1)} %get-tuple-element.289, f32[128]{0:T(128)S(1)} %get-tuple-element.286, ...), kind=kLoop, calls=%fused_computation.6.clone.1 | loop fusion | flops 1310720 | bytes 542212 | tf_op jit(solution)/shard_map/convert
  20.3 2.2 %fusion.189 = (bf16[1024,128]{0,1:T(8,128)(2,1)S(1)}, bf16[1024,128]{0,1:T(8,128)(2,1)S(1)}) fusion(f32[128]{0:T(128)S(1)} %get-tuple-element.290, f32[1024]{0:T(1024)S(1)} %get-tuple-element.291, f32[128]{0:T(128)S(1)} %get-tuple-element.288, f32[1024]{0:T(1024)S(1)} %get-tuple-element.289, f32[128]{0:T(128)S(1)} %get-tuple-element.286, ...), kind=kLoop, calls=%fused_computation.6.clone.1 | loop fusion | flops 1310720 | bytes 542212 | tf_op jit(solution)/shard_map/convert
  24.8 2.2 %fusion.189 = (bf16[1024,128]{0,1:T(8,128)(2,1)S(1)}, bf16[1024,128]{0,1:T(8,128)(2,1)S(1)}) fusion(f32[128]{0:T(128)S(1)} %get-tuple-element.290, f32[1024]{0:T(1024)S(1)} %get-tuple-element.291, f32[128]{0:T(128)S(1)} %get-tuple-element.288, f32[1024]{0:T(1024)S(1)} %get-tuple-element.289, f32[128]{0:T(128)S(1)} %get-tuple-element.286, ...), kind=kLoop, calls=%fused_computation.6.clone.1 | loop fusion | flops 1310720 | bytes 542212 | tf_op jit(solution)/shard_map/convert
  29.3 2.2 %fusion.189 = (bf16[1024,128]{0,1:T(8,128)(2,1)S(1)}, bf16[1024,128]{0,1:T(8,128)(2,1)S(1)}) fusion(f32[128]{0:T(128)S(1)} %get-tuple-element.290, f32[1024]{0:T(1024)S(1)} %get-tuple-element.291, f32[128]{0:T(128)S(1)} %get-tuple-element.288, f32[1024]{0:T(1024)S(1)} %get-tuple-element.289, f32[128]{0:T(128)S(1)} %get-tuple-element.286, ...), kind=kLoop, calls=%fused_computation.6.clone.1 | loop fusion | flops 1310720 | bytes 542212 | tf_op jit(solution)/shard_map/convert
  33.7 2.2 %fusion.189 = (bf16[1024,128]{0,1:T(8,128)(2,1)S(1)}, bf16[1024,128]{0,1:T(8,128)(2,1)S(1)}) fusion(f32[128]{0:T(128)S(1)} %get-tuple-element.290, f32[1024]{0:T(1024)S(1)} %get-tuple-element.291, f32[128]{0:T(128)S(1)} %get-tuple-element.288, f32[1024]{0:T(1024)S(1)} %get-tuple-element.289, f32[128]{0:T(128)S(1)} %get-tuple-element.286, ...), kind=kLoop, calls=%fused_computation.6.clone.1 | loop fusion | flops 1310720 | bytes 542212 | tf_op jit(solution)/shard_map/convert
  38.2 2.2 %fusion.189 = (bf16[1024,128]{0,1:T(8,128)(2,1)S(1)}, bf16[1024,128]{0,1:T(8,128)(2,1)S(1)}) fusion(f32[128]{0:T(128)S(1)} %get-tuple-element.290, f32[1024]{0:T(1024)S(1)} %get-tuple-element.291, f32[128]{0:T(128)S(1)} %get-tuple-element.288, f32[1024]{0:T(1024)S(1)} %get-tuple-element.289, f32[128]{0:T(128)S(1)} %get-tuple-element.286, ...), kind=kLoop, calls=%fused_computation.6.clone.1 | loop fusion | flops 1310720 | bytes 542212 | tf_op jit(solution)/shard_map/convert
  42.7 2.2 %fusion.189 = (bf16[1024,128]{0,1:T(8,128)(2,1)S(1)}, bf16[1024,128]{0,1:T(8,128)(2,1)S(1)}) fusion(f32[128]{0:T(128)S(1)} %get-tuple-element.290, f32[1024]{0:T(1024)S(1)} %get-tuple-element.291, f32[128]{0:T(128)S(1)} %get-tuple-element.288, f32[1024]{0:T(1024)S(1)} %get-tuple-element.289, f32[128]{0:T(128)S(1)} %get-tuple-element.286, ...), kind=kLoop, calls=%fused_computation.6.clone.1 | loop fusion | flops 1310720 | bytes 542212 | tf_op jit(solution)/shard_map/convert
  47.2 2.2 %fusion.189 = (bf16[1024,128]{0,1:T(8,128)(2,1)S(1)}, bf16[1024,128]{0,1:T(8,128)(2,1)S(1)}) fusion(f32[128]{0:T(128)S(1)} %get-tuple-element.290, f32[1024]{0:T(1024)S(1)} %get-tuple-element.291, f32[128]{0:T(128)S(1)} %get-tuple-element.288, f32[1024]{0:T(1024)S(1)} %get-tuple-element.289, f32[128]{0:T(128)S(1)} %get-tuple-element.286, ...), kind=kLoop, calls=%fused_computation.6.clone.1 | loop fusion | flops 1310720 | bytes 542212 | tf_op jit(solution)/shard_map/convert
  51.6 2.2 %fusion.189 = (bf16[1024,128]{0,1:T(8,128)(2,1)S(1)}, bf16[1024,128]{0,1:T(8,128)(2,1)S(1)}) fusion(f32[128]{0:T(128)S(1)} %get-tuple-element.290, f32[1024]{0:T(1024)S(1)} %get-tuple-element.291, f32[128]{0:T(128)S(1)} %get-tuple-element.288, f32[1024]{0:T(1024)S(1)} %get-tuple-element.289, f32[128]{0:T(128)S(1)} %get-tuple-element.286, ...), kind=kLoop, calls=%fused_computation.6.clone.1 | loop fusion | flops 1310720 | bytes 542212 | tf_op jit(solution)/shard_map/convert
  56.1 2.2 %fusion.189 = (bf16[1024,128]{0,1:T(8,128)(2,1)S(1)}, bf16[1024,128]{0,1:T(8,128)(2,1)S(1)}) fusion(f32[128]{0:T(128)S(1)} %get-tuple-element.290, f32[1024]{0:T(1024)S(1)} %get-tuple-element.291, f32[128]{0:T(128)S(1)} %get-tuple-element.288, f32[1024]{0:T(1024)S(1)} %get-tuple-element.289, f32[128]{0:T(128)S(1)} %get-tuple-element.286, ...), kind=kLoop, calls=%fused_computation.6.clone.1 | loop fusion | flops 1310720 | bytes 542212 | tf_op jit(solution)/shard_map/convert
  60.6 2.2 %fusion.189 = (bf16[1024,128]{0,1:T(8,128)(2,1)S(1)}, bf16[1024,128]{0,1:T(8,128)(2,1)S(1)}) fusion(f32[128]{0:T(128)S(1)} %get-tuple-element.290, f32[1024]{0:T(1024)S(1)} %get-tuple-element.291, f32[128]{0:T(128)S(1)} %get-tuple-element.288, f32[1024]{0:T(1024)S(1)} %get-tuple-element.289, f32[128]{0:T(128)S(1)} %get-tuple-element.286, ...), kind=kLoop, calls=%fused_computation.6.clone.1 | loop fusion | flops 1310720 | bytes 542212 | tf_op jit(solution)/shard_map/convert
  65.0 2.2 %fusion.189 = (bf16[1024,128]{0,1:T(8,128)(2,1)S(1)}, bf16[1024,128]{0,1:T(8,128)(2,1)S(1)}) fusion(f32[128]{0:T(128)S(1)} %get-tuple-element.290, f32[1024]{0:T(1024)S(1)} %get-tuple-element.291, f32[128]{0:T(128)S(1)} %get-tuple-element.288, f32[1024]{0:T(1024)S(1)} %get-tuple-element.289, f32[128]{0:T(128)S(1)} %get-tuple-element.286, ...), kind=kLoop, calls=%fused_computation.6.clone.1 | loop fusion | flops 1310720 | bytes 542212 | tf_op jit(solution)/shard_map/convert
  67.3 1.4 %fusion.190 = f32[2,2,32,2,128]{4,2,3,1,0:T(8,128)S(1)} fusion(bf16[2,128,1024,1,1]{2,1,0,4,3:T(8,128)(2,1)S(1)} %bitcast.78, s32[16,2,2,32,1024]{4,3,2,1,0:T(8,128)} %get-tuple-element.284, s32[]{:T(128)S(6)} %copy.19), kind=kOutput, calls=%fused_computation.10.clone.1 | convolution fusion | flops 67239936 | bytes 1179652 | tf_op jit(solution)/shard_map/while/body/eval_jaxpr/dot_general | solution.py:30
  69.5 2.2 %fusion.189 = (bf16[1024,128]{0,1:T(8,128)(2,1)S(1)}, bf16[1024,128]{0,1:T(8,128)(2,1)S(1)}) fusion(f32[128]{0:T(128)S(1)} %get-tuple-element.290, f32[1024]{0:T(1024)S(1)} %get-tuple-element.291, f32[128]{0:T(128)S(1)} %get-tuple-element.288, f32[1024]{0:T(1024)S(1)} %get-tuple-element.289, f32[128]{0:T(128)S(1)} %get-tuple-element.286, ...), kind=kLoop, calls=%fused_computation.6.clone.1 | loop fusion | flops 1310720 | bytes 542212 | tf_op jit(solution)/shard_map/convert
  71.8 1.4 %fusion.190 = f32[2,2,32,2,128]{4,2,3,1,0:T(8,128)S(1)} fusion(bf16[2,128,1024,1,1]{2,1,0,4,3:T(8,128)(2,1)S(1)} %bitcast.78, s32[16,2,2,32,1024]{4,3,2,1,0:T(8,128)} %get-tuple-element.284, s32[]{:T(128)S(6)} %copy.19), kind=kOutput, calls=%fused_computation.10.clone.1 | convolution fusion | flops 67239936 | bytes 1179652 | tf_op jit(solution)/shard_map/while/body/eval_jaxpr/dot_general | solution.py:30
  74.1 1.8 %reshape.148 = bf16[16,2,2048]{2,1,0:T(2,128)(2,1)} reshape(bf16[16,16,16,16]{3,2,1,0:T(8,128)(2,1)S(1)} %bitcast.81) | data formatting | bytes 262144
  75.8 7.4 %all-to-all-start = ((bf16[16,2,2048]{2,1,0:T(2,128)(2,1)}), bf16[16,2,2048]{2,1,0:T(2,128)(2,1)S(1)}, u32[]{:S(2)}, u32[]{:S(2)}) async-start(bf16[16,2,2048]{2,1,0:T(2,128)(2,1)} %reshape.148), calls=%async_computation | async-start | bytes 262144 | tf_op jit(solution)/shard_map/all_to_all | solution.py:91
  83.3 7.8 %all-to-all-done = bf16[16,2,2048]{2,1,0:T(2,128)(2,1)S(1)} async-done(((bf16[16,2,2048]{2,1,0:T(2,128)(2,1)}), bf16[16,2,2048]{2,1,0:T(2,128)(2,1)S(1)}, u32[]{:S(2)}, u32[]{:S(2)}) %all-to-all-start) | async-done | bytes 131104 | tf_op jit(solution)/shard_map/all_to_all | solution.py:91
  95.4 8.3 %collective-permute-done = bf16[256,15,16]{0,2,1:T(8,128)(2,1)S(1)} collective-permute-done((bf16[256,15,16]{0,2,1:T(8,128)(2,1)S(1)}, bf16[256,15,16]{0,2,1:T(8,128)(2,1)S(1)}, u32[]{:S(2)}, u32[]{:S(2)}) %collective-permute-start) | collective-permute-done | bytes 122912 | tf_op jit(solution)/shard_map/ppermute | solution.py:15
  (141 shorter events, 46.0 us)
Async XLA Ops:
  1.6 93.3 %copy-start = (s32[256]{0:T(256)S(1)}, s32[256]{0:T(256)}, u32[]{:S(2)}) copy-start(s32[256]{0:T(256)} %param.11) | copy-start | bytes 3076
  75.8 15.3 %all-to-all-start = ((bf16[16,2,2048]{2,1,0:T(2,128)(2,1)}), bf16[16,2,2048]{2,1,0:T(2,128)(2,1)S(1)}, u32[]{:S(2)}, u32[]{:S(2)}) async-start(bf16[16,2,2048]{2,1,0:T(2,128)(2,1)} %reshape.148), calls=%async_computation | async-start | bytes 262144 | tf_op jit(solution)/shard_map/all_to_all | solution.py:91
  93.7 10.0 %collective-permute-start = (bf16[256,15,16]{0,2,1:T(8,128)(2,1)S(1)}, bf16[256,15,16]{0,2,1:T(8,128)(2,1)S(1)}, u32[]{:S(2)}, u32[]{:S(2)}) collective-permute-start(bf16[256,15,16]{0,2,1:T(8,128)(2,1)S(1)} %slice.144), channel_id=1, source_target_pairs={{8,0},{9,1},{10,2},{11,3},{12,4},{13,5},{14,6},{15,7},{24,16},{25,... | collective-permute-start | bytes 368648 | tf_op jit(solution)/shard_map/ppermute | solution.py:15
where the time goes:
time: 113 us; the launch traced here: 111 us
  other arithmetic  49.3 us (44%)
  matrix products  28.6 us (25%)
  waiting for transfers between devices  16.1 us (14%)
  starting transfers between devices  8.67 us (8%)
  local copies, waits for them, and re-layouts  7.75 us (7%)
    another operation x16, other arithmetic  35.1 us
    dot_general x16, matrix products, channel_flat(): jnp.dot(row_block, weight_pair, preferred_element_type=jnp.float32)  21.7 us
    convert_element_type x16, other arithmetic, channel_flat(): scale_col = scale_chan.astype(jnp.float32)[:, None]  12.3 us
    ppermute x1, waiting for transfers between devices, passed_along(): lax.ppermute(value, axis, [(source, source + steps) for source in range(l...  8.26 us
    all_to_all x1, waiting for transfers between devices, local(): lax.all_to_all(outgoing, 'chan', split_axis=0, concat_axis=0, tiled=True)  7.81 us
    all_to_all x1, starting transfers between devices, local(): lax.all_to_all(outgoing, 'chan', split_axis=0, concat_axis=0, tiled=True)  7.38 us
    dot_general x16, matrix products, dedisperse(): jnp.dot(onehots[shift_step], segment, preferred_element_type=jnp.float32)  6.9 us
    unnamed x4, local copies, waits for them, and re-layouts  2.46 us
  transfers between devices with their start and end apart: 2, of which 2 were waited for; matrix products, arithmetic and copies ran while one was open for 0% of the time, Pallas kernels for 0%

commit v1 on v0

--- a/solution.py
+++ b/solution.py
@@ -7,6 +7,17 @@
 MAXD = 15
 TWO_PI = 6.283185307179586
 POWER_SCALE = 1.0 / 67108864.0
+
+
+def in_blocks(value, dim, size):
+    before, after = (value.shape[:dim], value.shape[dim + 1 :])
+    return jnp.moveaxis(value.reshape(*before, size, -1, *after), dim, 0)
+
+
+def in_order(pieces, dim):
+    shape = list(pieces.shape[1:])
+    shape[dim] *= pieces.shape[0]
+    return jnp.moveaxis(pieces, 0, dim).reshape(shape)
 
 
 def passed_along(value, axis, steps):
@@ -88,7 +99,14 @@
     outgoing = outgoing.transpose(1, 3, 0, 2, 4).reshape(
         groups, chan_local, time_steps, block_beams
     )
-    arrived = lax.all_to_all(outgoing, "chan", split_axis=0, concat_axis=0, tiled=True)
+    length, here = (lax.axis_size("chan"), lax.axis_index("chan"))
+    tiles = in_blocks(outgoing, 0, length)
+    done = [tiles[here]]
+    for lap in range(1, length):
+        sent = tiles[here ^ lap]
+        done.append(lax.ppermute(sent, "chan", [(i, i ^ lap) for i in range(length)]))
+    tiles = jnp.stack(done)[here ^ jnp.arange(length)]
+    arrived = in_order(tiles, 0)
     arrived_block = arrived.reshape(chan_total, time_steps, arrived.shape[3])
     tail_rows = passed_along(arrived_block[:, :MAXD, :], "chan", -half_groups)
     extended = jnp.concatenate([arrived_block, tail_rows], axis=1)

time: 113 us -> 132 us (1.17)
  starting transfers between devices: 8.67 us -> 26.9 us
  waiting for transfers between devices: 16.1 us -> 17.7 us
    ppermute x0 -> x15, starting transfers between devices: none -> 25.4 us  [local(): lax.ppermute(sent, 'chan', [(i, i ^ lap) for i in range(length)])]
    all_to_all x1 -> x0, waiting for transfers between devices: 7.81 us -> none  [local(): lax.all_to_all(outgoing, 'chan', split_axis=0, concat_axis=0, tiled=True)]
    ppermute x0 -> x15, waiting for transfers between devices: none -> 7.55 us  [local(): lax.ppermute(sent, 'chan', [(i, i ^ lap) for i in range(length)])]
    all_to_all x1 -> x0, starting transfers between devices: 7.38 us -> none  [local(): lax.all_to_all(outgoing, 'chan', split_axis=0, concat_axis=0, tiled=True)]
    unnamed x4 -> x16, local copies, waits for them, and re-layouts: 2.46 us -> 0.19 us
    ppermute x1, waiting for transfers between devices: 8.26 us -> 10.1 us  [passed_along(): lax.ppermute(value, axis, [(source, source + steps) for source in range(l...]
  transfers between devices with their start and end apart: 2 -> 16, of which waited for: 2 -> 4; matrix products, arithmetic and copies ran while one was open for 0% -> 1% of each run, Pallas kernels for 0% -> 0%
where the time goes in v1:
time: 132 us; the launch traced here: 130 us
  other arithmetic  49.3 us (37%)
  matrix products  28.6 us (22%)
  starting transfers between devices  26.9 us (20%)
  waiting for transfers between devices  17.7 us (13%)
  local copies, waits for them, and re-layouts  6.53 us (5%)
    another operation x16, other arithmetic  35.1 us
    ppermute x15, starting transfers between devices, local(): lax.ppermute(sent, 'chan', [(i, i ^ lap) for i in range(length)])  25.4 us
    dot_general x16, matrix products, channel_flat(): jnp.dot(row_block, weight_pair, preferred_element_type=jnp.float32)  21.7 us
    convert_element_type x16, other arithmetic, channel_flat(): scale_col = scale_chan.astype(jnp.float32)[:, None]  12.3 us
    ppermute x1, waiting for transfers between devices, passed_along(): lax.ppermute(value, axis, [(source, source + steps) for source in range(l...  10.1 us
    ppermute x15, waiting for transfers between devices, local(): lax.ppermute(sent, 'chan', [(i, i ^ lap) for i in range(length)])  7.55 us
    dot_general x16, matrix products, dedisperse(): jnp.dot(onehots[shift_step], segment, preferred_element_type=jnp.float32)  6.9 us
  transfers between devices with their start and end apart: 16, of which 4 were waited for; matrix products, arithmetic and copies ran while one was open for 1% of the time, Pallas kernels for 0%

profile of v1, /device:TPU:0, one launch (start us, length us, event | category | flops | bytes accessed | tf_op | source)
XLA Modules:
  0.0 130.1 jit_solution(9538436267019791826)
XLA Ops:
  1.6 71.5 %while.12 = (s32[]{:T(128)}, bf16[16,32,128]{2,1,0:T(8,128)(2,1)S(1)}, s32[16,2,2,32,1024]{4,3,2,1,0:T(8,128)}, s32[16,1024]{1,0:T(8,128)}, f32[128]{0:T(128)S(1...) while((s32[]{:T(128)}, ...), condition=%wide.region_2.3_spmd.clone.clone, body=%wide.region_0.2_spmd.clone.clone.sunk | while | flops 69661696 | bytes 3083917 | solution.py:95
  2.4 2.2 %fusion.190 = (bf16[1024,128]{0,1:T(8,128)(2,1)S(1)}, bf16[1024,128]{0,1:T(8,128)(2,1)S(1)}) fusion(f32[128]{0:T(128)S(1)} %get-tuple-element.306, f32[1024]{0:T(1024)S(1)} %get-tuple-element.307, f32[128]{0:T(128)S(1)} %get-tuple-element.304, f32[1024]{0:T(1024)S(1)} %get-tuple-element.305, f32[128]{0:T(128)S(1)} %get-tuple-element.302, ...), kind=kLoop, calls=%fused_computation.7.clone.1 | loop fusion | flops 1310720 | bytes 542212 | tf_op jit(solution)/shard_map/convert
  6.9 2.2 %fusion.190 = (bf16[1024,128]{0,1:T(8,128)(2,1)S(1)}, bf16[1024,128]{0,1:T(8,128)(2,1)S(1)}) fusion(f32[128]{0:T(128)S(1)} %get-tuple-element.306, f32[1024]{0:T(1024)S(1)} %get-tuple-element.307, f32[128]{0:T(128)S(1)} %get-tuple-element.304, f32[1024]{0:T(1024)S(1)} %get-tuple-element.305, f32[128]{0:T(128)S(1)} %get-tuple-element.302, ...), kind=kLoop, calls=%fused_computation.7.clone.1 | loop fusion | flops 1310720 | bytes 542212 | tf_op jit(solution)/shard_map/convert
  11.4 2.2 %fusion.190 = (bf16[1024,128]{0,1:T(8,128)(2,1)S(1)}, bf16[1024,128]{0,1:T(8,128)(2,1)S(1)}) fusion(f32[128]{0:T(128)S(1)} %get-tuple-element.306, f32[1024]{0:T(1024)S(1)} %get-tuple-element.307, f32[128]{0:T(128)S(1)} %get-tuple-element.304, f32[1024]{0:T(1024)S(1)} %get-tuple-element.305, f32[128]{0:T(128)S(1)} %get-tuple-element.302, ...), kind=kLoop, calls=%fused_computation.7.clone.1 | loop fusion | flops 1310720 | bytes 542212 | tf_op jit(solution)/shard_map/convert
  20.3 2.2 %fusion.190 = (bf16[1024,128]{0,1:T(8,128)(2,1)S(1)}, bf16[1024,128]{0,1:T(8,128)(2,1)S(1)}) fusion(f32[128]{0:T(128)S(1)} %get-tuple-element.306, f32[1024]{0:T(1024)S(1)} %get-tuple-element.307, f32[128]{0:T(128)S(1)} %get-tuple-element.304, f32[1024]{0:T(1024)S(1)} %get-tuple-element.305, f32[128]{0:T(128)S(1)} %get-tuple-element.302, ...), kind=kLoop, calls=%fused_computation.7.clone.1 | loop fusion | flops 1310720 | bytes 542212 | tf_op jit(solution)/shard_map/convert
  24.8 2.2 %fusion.190 = (bf16[1024,128]{0,1:T(8,128)(2,1)S(1)}, bf16[1024,128]{0,1:T(8,128)(2,1)S(1)}) fusion(f32[128]{0:T(128)S(1)} %get-tuple-element.306, f32[1024]{0:T(1024)S(1)} %get-tuple-element.307, f32[128]{0:T(128)S(1)} %get-tuple-element.304, f32[1024]{0:T(1024)S(1)} %get-tuple-element.305, f32[128]{0:T(128)S(1)} %get-tuple-element.302, ...), kind=kLoop, calls=%fused_computation.7.clone.1 | loop fusion | flops 1310720 | bytes 542212 | tf_op jit(solution)/shard_map/convert
  33.7 2.2 %fusion.190 = (bf16[1024,128]{0,1:T(8,128)(2,1)S(1)}, bf16[1024,128]{0,1:T(8,128)(2,1)S(1)}) fusion(f32[128]{0:T(128)S(1)} %get-tuple-element.306, f32[1024]{0:T(1024)S(1)} %get-tuple-element.307, f32[128]{0:T(128)S(1)} %get-tuple-element.304, f32[1024]{0:T(1024)S(1)} %get-tuple-element.305, f32[128]{0:T(128)S(1)} %get-tuple-element.302, ...), kind=kLoop, calls=%fused_computation.7.clone.1 | loop fusion | flops 1310720 | bytes 542212 | tf_op jit(solution)/shard_map/convert
  38.2 2.2 %fusion.190 = (bf16[1024,128]{0,1:T(8,128)(2,1)S(1)}, bf16[1024,128]{0,1:T(8,128)(2,1)S(1)}) fusion(f32[128]{0:T(128)S(1)} %get-tuple-element.306, f32[1024]{0:T(1024)S(1)} %get-tuple-element.307, f32[128]{0:T(128)S(1)} %get-tuple-element.304, f32[1024]{0:T(1024)S(1)} %get-tuple-element.305, f32[128]{0:T(128)S(1)} %get-tuple-element.302, ...), kind=kLoop, calls=%fused_computation.7.clone.1 | loop fusion | flops 1310720 | bytes 542212 | tf_op jit(solution)/shard_map/convert
  42.7 2.2 %fusion.190 = (bf16[1024,128]{0,1:T(8,128)(2,1)S(1)}, bf16[1024,128]{0,1:T(8,128)(2,1)S(1)}) fusion(f32[128]{0:T(128)S(1)} %get-tuple-element.306, f32[1024]{0:T(1024)S(1)} %get-tuple-element.307, f32[128]{0:T(128)S(1)} %get-tuple-element.304, f32[1024]{0:T(1024)S(1)} %get-tuple-element.305, f32[128]{0:T(128)S(1)} %get-tuple-element.302, ...), kind=kLoop, calls=%fused_computation.7.clone.1 | loop fusion | flops 1310720 | bytes 542212 | tf_op jit(solution)/shard_map/convert
  51.6 2.2 %fusion.190 = (bf16[1024,128]{0,1:T(8,128)(2,1)S(1)}, bf16[1024,128]{0,1:T(8,128)(2,1)S(1)}) fusion(f32[128]{0:T(128)S(1)} %get-tuple-element.306, f32[1024]{0:T(1024)S(1)} %get-tuple-element.307, f32[128]{0:T(128)S(1)} %get-tuple-element.304, f32[1024]{0:T(1024)S(1)} %get-tuple-element.305, f32[128]{0:T(128)S(1)} %get-tuple-element.302, ...), kind=kLoop, calls=%fused_computation.7.clone.1 | loop fusion | flops 1310720 | bytes 542212 | tf_op jit(solution)/shard_map/convert
  56.1 2.2 %fusion.190 = (bf16[1024,128]{0,1:T(8,128)(2,1)S(1)}, bf16[1024,128]{0,1:T(8,128)(2,1)S(1)}) fusion(f32[128]{0:T(128)S(1)} %get-tuple-element.306, f32[1024]{0:T(1024)S(1)} %get-tuple-element.307, f32[128]{0:T(128)S(1)} %get-tuple-element.304, f32[1024]{0:T(1024)S(1)} %get-tuple-element.305, f32[128]{0:T(128)S(1)} %get-tuple-element.302, ...), kind=kLoop, calls=%fused_computation.7.clone.1 | loop fusion | flops 1310720 | bytes 542212 | tf_op jit(solution)/shard_map/convert
  60.5 2.2 %fusion.190 = (bf16[1024,128]{0,1:T(8,128)(2,1)S(1)}, bf16[1024,128]{0,1:T(8,128)(2,1)S(1)}) fusion(f32[128]{0:T(128)S(1)} %get-tuple-element.306, f32[1024]{0:T(1024)S(1)} %get-tuple-element.307, f32[128]{0:T(128)S(1)} %get-tuple-element.304, f32[1024]{0:T(1024)S(1)} %get-tuple-element.305, f32[128]{0:T(128)S(1)} %get-tuple-element.302, ...), kind=kLoop, calls=%fused_computation.7.clone.1 | loop fusion | flops 1310720 | bytes 542212 | tf_op jit(solution)/shard_map/convert
  65.0 2.2 %fusion.190 = (bf16[1024,128]{0,1:T(8,128)(2,1)S(1)}, bf16[1024,128]{0,1:T(8,128)(2,1)S(1)}) fusion(f32[128]{0:T(128)S(1)} %get-tuple-element.306, f32[1024]{0:T(1024)S(1)} %get-tuple-element.307, f32[128]{0:T(128)S(1)} %get-tuple-element.304, f32[1024]{0:T(1024)S(1)} %get-tuple-element.305, f32[128]{0:T(128)S(1)} %get-tuple-element.302, ...), kind=kLoop, calls=%fused_computation.7.clone.1 | loop fusion | flops 1310720 | bytes 542212 | tf_op jit(solution)/shard_map/convert
  69.5 2.2 %fusion.190 = (bf16[1024,128]{0,1:T(8,128)(2,1)S(1)}, bf16[1024,128]{0,1:T(8,128)(2,1)S(1)}) fusion(f32[128]{0:T(128)S(1)} %get-tuple-element.306, f32[1024]{0:T(1024)S(1)} %get-tuple-element.307, f32[128]{0:T(128)S(1)} %get-tuple-element.304, f32[1024]{0:T(1024)S(1)} %get-tuple-element.305, f32[128]{0:T(128)S(1)} %get-tuple-element.302, ...), kind=kLoop, calls=%fused_computation.7.clone.1 | loop fusion | flops 1310720 | bytes 542212 | tf_op jit(solution)/shard_map/convert
  74.9 2.6 %collective-permute-start.1 = (bf16[1,16,16,16]{3,2,1,0:T(8,128)(2,1)S(1)}, bf16[1,16,16,16]{3,2,1,0:T(8,128)(2,1)S(1)}, u32[]{:S(2)}, u32[]{:S(2)}) collective-permute-start(bf16[1,16,16,16]{3,2,1,0:T(8,128)(2,1)S(1)} %get-tuple-element.171), channel_id=1, source_target_pairs={{0,2},{1,3},{2,0},{3,1},{4,6},{5,7},{6,4},{7,5},{8,10},{9,11},{10,... | collective-permute-start | bytes 24584 | tf_op jit(solution)/shard_map/ppermute | solution.py:107
  79.6 2.7 %collective-permute-start.5 = (bf16[1,16,16,16]{3,2,1,0:T(8,128)(2,1)S(1)}, bf16[1,16,16,16]{3,2,1,0:T(8,128)(2,1)S(1)}, u32[]{:S(2)}, u32[]{:S(2)}) collective-permute-start(bf16[1,16,16,16]{3,2,1,0:T(8,128)(2,1)S(1)} %get-tuple-element.167), channel_id=1, source_target_pairs={{0,6},{1,7},{2,4},{3,5},{4,2},{5,3},{6,0},{7,1},{8,14},{9,15},{10,... | collective-permute-start | bytes 24584 | tf_op jit(solution)/shard_map/ppermute | solution.py:107
  82.4 2.7 %collective-permute-start.7 = (bf16[1,16,16,16]{3,2,1,0:T(8,128)(2,1)S(1)}, bf16[1,16,16,16]{3,2,1,0:T(8,128)(2,1)S(1)}, u32[]{:S(2)}, u32[]{:S(2)}) collective-permute-start(bf16[1,16,16,16]{3,2,1,0:T(8,128)(2,1)S(1)} %get-tuple-element.165), channel_id=1, source_target_pairs={{0,8},{1,9},{2,10},{3,11},{4,12},{5,13},{6,14},{7,15},{8,0},{9,1},... | collective-permute-start | bytes 24584 | tf_op jit(solution)/shard_map/ppermute | solution.py:107
  86.0 2.9 %collective-permute-start.9 = (bf16[1,16,16,16]{3,2,1,0:T(8,128)(2,1)S(1)}, bf16[1,16,16,16]{3,2,1,0:T(8,128)(2,1)S(1)}, u32[]{:S(2)}, u32[]{:S(2)}) collective-permute-start(bf16[1,16,16,16]{3,2,1,0:T(8,128)(2,1)S(1)} %get-tuple-element.163), channel_id=1, source_target_pairs={{0,10},{1,11},{2,8},{3,9},{4,14},{5,15},{6,12},{7,13},{8,2},{9,3},... | collective-permute-start | bytes 24584 | tf_op jit(solution)/shard_map/ppermute | solution.py:107
  89.4 3.3 %collective-permute-start.11 = (bf16[1,16,16,16]{3,2,1,0:T(8,128)(2,1)S(1)}, bf16[1,16,16,16]{3,2,1,0:T(8,128)(2,1)S(1)}, u32[]{:S(2)}, u32[]{:S(2)}) collective-permute-start(bf16[1,16,16,16]{3,2,1,0:T(8,128)(2,1)S(1)} %get-tuple-element.161), channel_id=1, source_target_pairs={{0,12},{1,13},{2,14},{3,15},{4,8},{5,9},{6,10},{7,11},{8,4},{9,5},... | collective-permute-start | bytes 24584 | tf_op jit(solution)/shard_map/ppermute | solution.py:107
  93.4 3.6 %collective-permute-done.8 = bf16[1,16,16,16]{3,2,1,0:T(8,128)(2,1)S(1)} collective-permute-done((bf16[1,16,16,16]{3,2,1,0:T(8,128)(2,1)S(1)}, bf16[1,16,16,16]{3,2,1,0:T(8,128)(2,1)S(1)}, u32[]{:S(2)}, u32[]{:S(2)}) %collective-permute-start.8) | collective-permute-done | bytes 8224 | tf_op jit(solution)/shard_map/ppermute | solution.py:107
  97.0 3.6 %collective-permute-start.13 = (bf16[1,16,16,16]{3,2,1,0:T(8,128)(2,1)S(1)}, bf16[1,16,16,16]{3,2,1,0:T(8,128)(2,1)S(1)}, u32[]{:S(2)}, u32[]{:S(2)}) collective-permute-start(bf16[1,16,16,16]{3,2,1,0:T(8,128)(2,1)S(1)} %get-tuple-element.159), channel_id=1, source_target_pairs={{0,14},{1,15},{2,12},{3,13},{4,10},{5,11},{6,8},{7,9},{8,6},{9,7},... | collective-permute-start | bytes 24584 | tf_op jit(solution)/shard_map/ppermute | solution.py:107
  100.9 3.1 %collective-permute-start.14 = (bf16[1,16,16,16]{3,2,1,0:T(8,128)(2,1)S(1)}, bf16[1,16,16,16]{3,2,1,0:T(8,128)(2,1)S(1)}, u32[]{:S(2)}, u32[]{:S(2)}) collective-permute-start(bf16[1,16,16,16]{3,2,1,0:T(8,128)(2,1)S(1)} %get-tuple-element.158), channel_id=1, source_target_pairs={{0,15},{1,14},{2,13},{3,12},{4,11},{5,10},{6,9},{7,8},{8,7},{9,6},... | collective-permute-start | bytes 24584 | tf_op jit(solution)/shard_map/ppermute | solution.py:107
  104.2 3.7 %collective-permute-done.14 = bf16[1,16,16,16]{3,2,1,0:T(8,128)(2,1)S(1)} collective-permute-done((bf16[1,16,16,16]{3,2,1,0:T(8,128)(2,1)S(1)}, bf16[1,16,16,16]{3,2,1,0:T(8,128)(2,1)S(1)}, u32[]{:S(2)}, u32[]{:S(2)}) %collective-permute-start.14) | collective-permute-done | bytes 8224 | tf_op jit(solution)/shard_map/ppermute | solution.py:107
  112.4 10.1 %collective-permute-done.15 = bf16[256,15,16]{0,2,1:T(8,128)(2,1)S(1)} collective-permute-done((bf16[256,15,16]{0,2,1:T(8,128)(2,1)S(1)}, bf16[256,15,16]{0,2,1:T(8,128)(2,1)S(1)}, u32[]{:S(2)}, u32[]{:S(2)}) %collective-permute-start.15) | collective-permute-done | bytes 122912 | tf_op jit(solution)/shard_map/ppermute | solution.py:26
  (186 shorter events, 62.0 us)
Async XLA Ops:
  73.2 38.8 %copy-start = (s32[256]{0:T(256)S(1)}, s32[256]{0:T(256)}, u32[]{:S(2)}) copy-start(s32[256]{0:T(256)} %param.11) | copy-start | bytes 3076
  74.4 5.1 %collective-permute-start = (bf16[1,16,16,16]{3,2,1,0:T(8,128)(2,1)S(1)}, bf16[1,16,16,16]{3,2,1,0:T(8,128)(2,1)S(1)}, u32[]{:S(2)}, u32[]{:S(2)}) collective-permute-start(bf16[1,16,16,16]{3,2,1,0:T(8,128)(2,1)S(1)} %get-tuple-element.172), channel_id=1, source_target_pairs={{0,1},{1,0},{2,3},{3,2},{4,5},{5,4},{6,7},{7,6},{8,9},{9,8},{10,11... | collective-permute-start | bytes 24584 | tf_op jit(solution)/shard_map/ppermute | solution.py:107
  74.9 7.3 %collective-permute-start.1 = (bf16[1,16,16,16]{3,2,1,0:T(8,128)(2,1)S(1)}, bf16[1,16,16,16]{3,2,1,0:T(8,128)(2,1)S(1)}, u32[]{:S(2)}, u32[]{:S(2)}) collective-permute-start(bf16[1,16,16,16]{3,2,1,0:T(8,128)(2,1)S(1)} %get-tuple-element.171), channel_id=1, source_target_pairs={{0,2},{1,3},{2,0},{3,1},{4,6},{5,7},{6,4},{7,5},{8,10},{9,11},{10,... | collective-permute-start | bytes 24584 | tf_op jit(solution)/shard_map/ppermute | solution.py:107
  77.5 4.9 %collective-permute-start.2 = (bf16[1,16,16,16]{3,2,1,0:T(8,128)(2,1)S(1)}, bf16[1,16,16,16]{3,2,1,0:T(8,128)(2,1)S(1)}, u32[]{:S(2)}, u32[]{:S(2)}) collective-permute-start(bf16[1,16,16,16]{3,2,1,0:T(8,128)(2,1)S(1)} %get-tuple-element.170), channel_id=1, source_target_pairs={{0,3},{1,2},{2,1},{3,0},{4,7},{5,6},{6,5},{7,4},{8,11},{9,10},{10,... | collective-permute-start | bytes 24584 | tf_op jit(solution)/shard_map/ppermute | solution.py:107
  77.6 7.6 %collective-permute-start.3 = (bf16[1,16,16,16]{3,2,1,0:T(8,128)(2,1)S(1)}, bf16[1,16,16,16]{3,2,1,0:T(8,128)(2,1)S(1)}, u32[]{:S(2)}, u32[]{:S(2)}) collective-permute-start(bf16[1,16,16,16]{3,2,1,0:T(8,128)(2,1)S(1)} %get-tuple-element.169), channel_id=1, source_target_pairs={{0,4},{1,5},{2,6},{3,7},{4,0},{5,1},{6,2},{7,3},{8,12},{9,13},{10,... | collective-permute-start | bytes 24584 | tf_op jit(solution)/shard_map/ppermute | solution.py:107
  79.4 6.6 %collective-permute-start.4 = (bf16[1,16,16,16]{3,2,1,0:T(8,128)(2,1)S(1)}, bf16[1,16,16,16]{3,2,1,0:T(8,128)(2,1)S(1)}, u32[]{:S(2)}, u32[]{:S(2)}) collective-permute-start(bf16[1,16,16,16]{3,2,1,0:T(8,128)(2,1)S(1)} %get-tuple-element.168), channel_id=1, source_target_pairs={{0,5},{1,4},{2,7},{3,6},{4,1},{5,0},{6,3},{7,2},{8,13},{9,12},{10,... | collective-permute-start | bytes 24584 | tf_op jit(solution)/shard_map/ppermute | solution.py:107
  79.6 9.4 %collective-permute-start.5 = (bf16[1,16,16,16]{3,2,1,0:T(8,128)(2,1)S(1)}, bf16[1,16,16,16]{3,2,1,0:T(8,128)(2,1)S(1)}, u32[]{:S(2)}, u32[]{:S(2)}) collective-permute-start(bf16[1,16,16,16]{3,2,1,0:T(8,128)(2,1)S(1)} %get-tuple-element.167), channel_id=1, source_target_pairs={{0,6},{1,7},{2,4},{3,5},{4,2},{5,3},{6,0},{7,1},{8,14},{9,15},{10,... | collective-permute-start | bytes 24584 | tf_op jit(solution)/shard_map/ppermute | solution.py:107
  82.3 7.1 %collective-permute-start.6 = (bf16[1,16,16,16]{3,2,1,0:T(8,128)(2,1)S(1)}, bf16[1,16,16,16]{3,2,1,0:T(8,128)(2,1)S(1)}, u32[]{:S(2)}, u32[]{:S(2)}) collective-permute-start(bf16[1,16,16,16]{3,2,1,0:T(8,128)(2,1)S(1)} %get-tuple-element.166), channel_id=1, source_target_pairs={{0,7},{1,6},{2,5},{3,4},{4,3},{5,2},{6,1},{7,0},{8,15},{9,14},{10,... | collective-permute-start | bytes 24584 | tf_op jit(solution)/shard_map/ppermute | solution.py:107
  82.4 10.3 %collective-permute-start.7 = (bf16[1,16,16,16]{3,2,1,0:T(8,128)(2,1)S(1)}, bf16[1,16,16,16]{3,2,1,0:T(8,128)(2,1)S(1)}, u32[]{:S(2)}, u32[]{:S(2)}) collective-permute-start(bf16[1,16,16,16]{3,2,1,0:T(8,128)(2,1)S(1)} %get-tuple-element.165), channel_id=1, source_target_pairs={{0,8},{1,9},{2,10},{3,11},{4,12},{5,13},{6,14},{7,15},{8,0},{9,1},... | collective-permute-start | bytes 24584 | tf_op jit(solution)/shard_map/ppermute | solution.py:107
  85.2 11.8 %collective-permute-start.8 = (bf16[1,16,16,16]{3,2,1,0:T(8,128)(2,1)S(1)}, bf16[1,16,16,16]{3,2,1,0:T(8,128)(2,1)S(1)}, u32[]{:S(2)}, u32[]{:S(2)}) collective-permute-start(bf16[1,16,16,16]{3,2,1,0:T(8,128)(2,1)S(1)} %get-tuple-element.164), channel_id=1, source_target_pairs={{0,9},{1,8},{2,11},{3,10},{4,13},{5,12},{6,15},{7,14},{8,1},{9,0},... | collective-permute-start | bytes 24584 | tf_op jit(solution)/shard_map/ppermute | solution.py:107
  86.0 14.9 %collective-permute-start.9 = (bf16[1,16,16,16]{3,2,1,0:T(8,128)(2,1)S(1)}, bf16[1,16,16,16]{3,2,1,0:T(8,128)(2,1)S(1)}, u32[]{:S(2)}, u32[]{:S(2)}) collective-permute-start(bf16[1,16,16,16]{3,2,1,0:T(8,128)(2,1)S(1)} %get-tuple-element.163), channel_id=1, source_target_pairs={{0,10},{1,11},{2,8},{3,9},{4,14},{5,15},{6,12},{7,13},{8,2},{9,3},... | collective-permute-start | bytes 24584 | tf_op jit(solution)/shard_map/ppermute | solution.py:107
  88.9 15.1 %collective-permute-start.10 = (bf16[1,16,16,16]{3,2,1,0:T(8,128)(2,1)S(1)}, bf16[1,16,16,16]{3,2,1,0:T(8,128)(2,1)S(1)}, u32[]{:S(2)}, u32[]{:S(2)}) collective-permute-start(bf16[1,16,16,16]{3,2,1,0:T(8,128)(2,1)S(1)} %get-tuple-element.162), channel_id=1, source_target_pairs={{0,11},{1,10},{2,9},{3,8},{4,15},{5,14},{6,13},{7,12},{8,3},{9,2},... | collective-permute-start | bytes 24584 | tf_op jit(solution)/shard_map/ppermute | solution.py:107
  89.4 14.7 %collective-permute-start.11 = (bf16[1,16,16,16]{3,2,1,0:T(8,128)(2,1)S(1)}, bf16[1,16,16,16]{3,2,1,0:T(8,128)(2,1)S(1)}, u32[]{:S(2)}, u32[]{:S(2)}) collective-permute-start(bf16[1,16,16,16]{3,2,1,0:T(8,128)(2,1)S(1)} %get-tuple-element.161), channel_id=1, source_target_pairs={{0,12},{1,13},{2,14},{3,15},{4,8},{5,9},{6,10},{7,11},{8,4},{9,5},... | collective-permute-start | bytes 24584 | tf_op jit(solution)/shard_map/ppermute | solution.py:107
  92.8 11.4 %collective-permute-start.12 = (bf16[1,16,16,16]{3,2,1,0:T(8,128)(2,1)S(1)}, bf16[1,16,16,16]{3,2,1,0:T(8,128)(2,1)S(1)}, u32[]{:S(2)}, u32[]{:S(2)}) collective-permute-start(bf16[1,16,16,16]{3,2,1,0:T(8,128)(2,1)S(1)} %get-tuple-element.160), channel_id=1, source_target_pairs={{0,13},{1,12},{2,15},{3,14},{4,9},{5,8},{6,11},{7,10},{8,5},{9,4},... | collective-permute-start | bytes 24584 | tf_op jit(solution)/shard_map/ppermute | solution.py:107
  97.0 7.1 %collective-permute-start.13 = (bf16[1,16,16,16]{3,2,1,0:T(8,128)(2,1)S(1)}, bf16[1,16,16,16]{3,2,1,0:T(8,128)(2,1)S(1)}, u32[]{:S(2)}, u32[]{:S(2)}) collective-permute-start(bf16[1,16,16,16]{3,2,1,0:T(8,128)(2,1)S(1)} %get-tuple-element.159), channel_id=1, source_target_pairs={{0,14},{1,15},{2,12},{3,13},{4,10},{5,11},{6,8},{7,9},{8,6},{9,7},... | collective-permute-start | bytes 24584 | tf_op jit(solution)/shard_map/ppermute | solution.py:107
  100.9 6.9 %collective-permute-start.14 = (bf16[1,16,16,16]{3,2,1,0:T(8,128)(2,1)S(1)}, bf16[1,16,16,16]{3,2,1,0:T(8,128)(2,1)S(1)}, u32[]{:S(2)}, u32[]{:S(2)}) collective-permute-start(bf16[1,16,16,16]{3,2,1,0:T(8,128)(2,1)S(1)} %get-tuple-element.158), channel_id=1, source_target_pairs={{0,15},{1,14},{2,13},{3,12},{4,11},{5,10},{6,9},{7,8},{8,7},{9,6},... | collective-permute-start | bytes 24584 | tf_op jit(solution)/shard_map/ppermute | solution.py:107
  110.5 12.0 %collective-permute-start.15 = (bf16[256,15,16]{0,2,1:T(8,128)(2,1)S(1)}, bf16[256,15,16]{0,2,1:T(8,128)(2,1)S(1)}, u32[]{:S(2)}, u32[]{:S(2)}) collective-permute-start(bf16[256,15,16]{0,2,1:T(8,128)(2,1)S(1)} %slice.146), channel_id=1, source_target_pairs={{8,0},{9,1},{10,2},{11,3},{12,4},{13,5},{14,6},{15,7},{24,16},{25,... | collective-permute-start | bytes 368648 | tf_op jit(solution)/shard_map/ppermute | solution.py:26
